TPU v7x, 32 devices: a whole 2x2x4 slice. The times are simulated.
32 devices in a mesh: dp: 8 (over z, core), tensor: 4 (over y, x).
Axes of the slice: x: 2, y: 2, z: 4, core: 2. Of those that a mesh axis runs over, the one named last changes fastest.
Arguments:
- hidden_in: bfloat16 [4096, 8192], P('dp', 'tensor'), may hold values from -6 to 6
- norm_gain: float32 [8192], P('tensor'), may hold values from 0.5 to 1.5
- key_weight: bfloat16 [8192, 512], P('tensor'), as said below
- value_weight: bfloat16 [8192, 512], P('tensor'), may hold values from -0.0625 to 0.0625
- queries: bfloat16 [4096, 4096], P('dp', 'tensor'), may hold values from -8 to 8
- segments: int32 [8, 512], P('dp'), may hold values from 0 to 3, never falling along the last dimension, each value on 1 to 256 neighbouring positions
- cotangent: bfloat16 [4096, 4096], P('dp', 'tensor'), may hold values from -6 to 6
Outputs:
- attn_out: bfloat16 [4096, 4096], P('dp', 'tensor')
- grad_hidden: bfloat16 [4096, 8192], P('dp', 'tensor')
- grad_queries: bfloat16 [4096, 4096], P('dp', 'tensor')
- grad_key_weight: float32 [8192, 512], P(('tensor', 'dp'))
- grad_value_weight: float32 [8192, 512], P(('tensor', 'dp'))
- grad_gain: float32 [8192], P(('tensor', 'dp'))
Inputs may be any that keep to these rules, and one draw needn't show every extreme that they name: `segments`: segment numbers never fall along a row; each document has 1 to 256 tokens, one exactly 256. `key_weight`: entries have a standard deviation of about 8192^(-1/2) and lie within 6 such deviations.
All inputs are finite; a program needn't handle non-finite values.
Results may differ from a plain program's by a relative error of at most 0.035.
Values may be sent and summed in bfloat16 or wider, within the bound.
A program may use at most 64 MiB of HBM per device.

v0:
```python
import jax
import jax.numpy as jnp
from jax import lax
from jax.sharding import PartitionSpec as P

D = 8192
HQ = 32
KVH = 4
HD = 128


ROPE_BASE = 500000.0


def angles(pos, head_size, ndim):
    half = head_size // 2
    freq = ROPE_BASE ** (-(jnp.arange(half).astype(jnp.float32) * 2.0 / head_size))
    angle = pos[:, None] * freq[None, :]
    shape = (pos.shape[0],) + (1,) * (ndim - 2) + (half,)
    return (jnp.cos(angle).reshape(shape), jnp.sin(angle).reshape(shape))


def rotate(vec, pos, sign):
    half = vec.shape[-1] // 2
    cosine, sine = angles(pos, vec.shape[-1], vec.ndim)
    first = vec[..., :half]
    second = vec[..., half:]
    return jnp.concatenate(
        [first * cosine - sign * second * sine, second * cosine + sign * first * sine], axis=-1
    )


def row_layout(seg):
    rows = seg.shape[0]
    index = jnp.arange(rows)
    same = seg[:, None] == seg[None, :]
    start = jnp.min(jnp.where(same, index[None, :], rows), axis=1)
    pos = (index - start).astype(jnp.float32)
    allowed = same & (index[None, :] <= index[:, None])
    return (pos, allowed)


def body(hidden_in, norm_gain, key_weight, value_weight, queries, segments, cotangent):
    rows = hidden_in.shape[0]
    width = key_weight.shape[1]
    group = HQ // KVH
    scale = 1.0 / HD**0.5
    tens_size = lax.axis_size("tensor")
    tens_index = lax.axis_index("tensor")
    local_heads = queries.shape[1] // HD
    kv_count = max(local_heads // group, 1)
    repeat = min(local_heads, group)
    kv_first = tens_index * local_heads // group
    sharers = max(tens_size // KVH, 1)
    in_float = hidden_in.astype(jnp.float32)
    square_sum = lax.psum(jnp.sum(in_float * in_float, axis=1), "tensor")
    inv_rms = lax.rsqrt(square_sum / D + 1e-05)
    unit = in_float * inv_rms[:, None]
    normed = (unit * norm_gain[None, :]).astype(jnp.bfloat16)
    partial_value = jnp.stack(
        [
            jnp.dot(normed, key_weight, preferred_element_type=jnp.float32),
            jnp.dot(normed, value_weight, preferred_element_type=jnp.float32),
        ],
        axis=1,
    )
    kv_both = lax.psum(partial_value.reshape(rows, 2 * width), "tensor").astype(jnp.bfloat16)
    kv_heads = kv_both.reshape(rows, 2, KVH, HD)
    key_local = lax.dynamic_slice_in_dim(kv_heads[:, 0], kv_first, kv_count, 1)
    value_local = lax.dynamic_slice_in_dim(kv_heads[:, 1], kv_first, kv_count, 1)
    pos, allowed = row_layout(segments[0])
    query_four = queries.reshape(rows, kv_count, repeat, HD)
    q_rot = rotate(query_four.astype(jnp.float32), pos, 1.0).astype(jnp.bfloat16)
    k_rot = rotate(key_local.astype(jnp.float32), pos, 1.0).astype(jnp.bfloat16)
    scores = jnp.einsum("qcrd,kcd->crqk", q_rot, k_rot, preferred_element_type=jnp.float32) * scale
    scores = jnp.where(allowed[None, None], scores, -1e30)
    top = jnp.max(scores, axis=-1, keepdims=True)
    expo = jnp.exp(scores - top)
    probs = (expo / jnp.sum(expo, axis=-1, keepdims=True)).astype(jnp.bfloat16)
    attn_out = (
        jnp.einsum("crqk,kcd->qcrd", probs, value_local, preferred_element_type=jnp.float32)
        .astype(jnp.bfloat16)
        .reshape(rows, local_heads * HD)
    )
    cot_four = cotangent.reshape(rows, kv_count, repeat, HD)
    d_probs = jnp.einsum(
        "qcrd,kcd->crqk", cot_four, value_local, preferred_element_type=jnp.float32
    )
    prob_float = probs.astype(jnp.float32)
    delta = jnp.sum(prob_float * d_probs, axis=-1, keepdims=True)
    d_scores = (prob_float * (d_probs - delta) * scale).astype(jnp.bfloat16)
    d_qrot = jnp.einsum("crqk,kcd->qcrd", d_scores, k_rot, preferred_element_type=jnp.float32)
    grad_queries = rotate(d_qrot, pos, -1.0).astype(jnp.bfloat16).reshape(rows, local_heads * HD)
    d_krot = jnp.einsum("crqk,qcrd->kcd", d_scores, q_rot, preferred_element_type=jnp.float32)
    d_key_part = rotate(d_krot, pos, -1.0)
    d_value_part = jnp.einsum("crqk,qcrd->kcd", probs, cot_four, preferred_element_type=jnp.float32)
    grad_part = jnp.stack([d_key_part, d_value_part], axis=1)
    gathered = lax.all_gather(grad_part.astype(jnp.bfloat16), "tensor", axis=2, tiled=True).astype(
        grad_part.dtype
    )
    summed = jnp.sum(gathered.reshape(rows, 2, KVH, sharers, HD), axis=3)
    kv_grad = summed.astype(jnp.bfloat16).reshape(rows, 2, width)
    d_keys = kv_grad[:, 0]
    d_values = kv_grad[:, 1]
    d_normed = jnp.dot(d_keys, key_weight.T, preferred_element_type=jnp.float32) + jnp.dot(
        d_values, value_weight.T, preferred_element_type=jnp.float32
    )
    key_term = jnp.dot(normed.T, d_keys, preferred_element_type=jnp.float32)
    value_term = jnp.dot(normed.T, d_values, preferred_element_type=jnp.float32)
    gain_term = jnp.sum(d_normed * unit, axis=0)
    grad_key, grad_value, grad_gain = (
        lax.psum_scatter(
            key_term.astype(jnp.bfloat16), "dp", scatter_dimension=0, tiled=True
        ).astype(jnp.float32),
        lax.psum_scatter(
            value_term.astype(jnp.bfloat16), "dp", scatter_dimension=0, tiled=True
        ).astype(jnp.float32),
        lax.psum_scatter(
            gain_term.astype(jnp.bfloat16), "dp", scatter_dimension=0, tiled=True
        ).astype(jnp.float32),
    )
    d_unit = d_normed * norm_gain[None, :]
    corr = lax.psum(jnp.sum(d_unit * unit, axis=1), "tensor") / D
    grad_hidden = (inv_rms[:, None] * (d_unit - unit * corr[:, None])).astype(jnp.bfloat16)
    return (attn_out, grad_hidden, grad_queries, grad_key, grad_value, grad_gain)


def solution(mesh):
    return jax.shard_map(
        body,
        mesh=mesh,
        in_specs=(
            P("dp", "tensor"),
            P("tensor"),
            P("tensor", None),
            P("tensor", None),
            P("dp", "tensor"),
            P("dp", None),
            P("dp", "tensor"),
        ),
        out_specs=(
            P("dp", "tensor"),
            P("dp", "tensor"),
            P("dp", "tensor"),
            P(("tensor", "dp"), None),
            P(("tensor", "dp"), None),
            P(("tensor", "dp")),
        ),
        check_vma=False,
    )
```

profile of v0, /device:TPU:0, one launch (start us, length us, event | category | flops | bytes accessed | tf_op | source)
XLA Modules:
  0.0 255.4 jit_solution(414304127542360610)
XLA Ops:
  9.3 2.1 fusion.15
  11.4 11.4 %psum.21 = f32[512]{0:T(512)S(1)} all-reduce(f32[512]{0:T(512)S(1)} %fusion.15), channel_id=1, replica_groups=mesh['dp'=8,'tensor'=4] {'tensor'}, use_global_device_ids=true, to_apply=%region_1.2 | all-reduce | flops 512 | bytes 4096 | tf_op jit(solution)/shard_map/psum | solution.py:56
  22.8 3.1 %convolution_bitcast_fusion.1 = f32[512,1,512]{0,2,1:T(8,128)S(1)} fusion(bf16[2048,512]{1,0:T(8,128)(2,1)S(1)} %copy-done, bf16[512,2048]{1,0:T(8,128)(2,1)} %param.7, f32[2048]{0:T(1024)} %param.8, f32[512]{0:T(512)S(1)} %add_rsqrt_fusion), kind=kOutput, calls=%fused_computation.39 | convolution fusion | flops 1077936128 | bytes 5253120 | tf_op jit(solution)/shard_map/dot_general | solution.py:63
  28.9 71.8 %all-reduce.2 = bf16[512,1024]{0,1:T(8,128)(2,1)S(1)} all-reduce(f32[512,1024]{0,1:T(8,128)} %bitcast.143), channel_id=1, replica_groups=mesh['dp'=8,'tensor'=4] {'tensor'}, use_global_device_ids=true, to_apply=%region_2.3 | all-reduce | flops 524288 | bytes 3145728 | tf_op jit(solution)/shard_map/psum | solution.py:67
  102.9 1.9 broadcast_multiply_fusion
  104.7 2.5 fusion.62
  108.7 1.6 fusion.75
  110.3 3.2 %copy.79 = f32[512,1,8,64]{3,0,2,1:T(8,128)} copy(f32[512,1,8,64]{0,3,2,1:T(8,128)} %get-tuple-element.35) | data formatting | bytes 2097152
  113.5 3.2 %copy.80 = f32[512,1,8,64]{3,0,2,1:T(8,128)} copy(f32[512,1,8,64]{0,3,2,1:T(8,128)} %get-tuple-element.34) | data formatting | bytes 2097152
  116.7 2.8 %fusion.34 = (bf16[512,8,64]{2,0,1:T(8,128)(2,1)S(1)}, bf16[512,8,64]{2,0,1:T(8,128)(2,1)S(1)}) fusion(f32[512,1,8,64]{3,0,2,1:T(8,128)} %copy.80, f32[512,1,8,64]{3,0,2,1:T(8,128)} %copy.79, f32[512,64]{1,0:T(8,128)S(1)} %copy-done.10, f32[512,64]{1,0:T(8,128)S(1)} %copy-done.5), kind=kLoop, calls=%fused_computation.48 | loop fusion | flops 2097152 | bytes 3407872 | tf_op jit(solution)/shard_map/concatenate | solution.py:28
  119.5 2.3 fusion.4
  121.8 1.8 fusion.3
  123.6 6.2 %fusion = (f32[8,512]{1,0:T(8,128)S(1)}, bf16[1,8,512,512]{2,3,1,0:T(8,128)(2,1)S(1)}, f32[512,512,8]{1,0,2:T(8,128)}) fusion(f32[8,512]{1,0:T(8,128)S(1)} %fusion.3, f32[8,512]{1,0:T(8,128)S(1)} %get-tuple-element.43, f32[512,512,8]{1,0,2:T(8,128)S(1)} %get-tuple-element.44, pred[512,512]{0,1:T(8,128)(4,1)S(1)} %compare_and_fusion, ...), kind=kOutput, calls=%fused_computation.2 | convolution fusion | flops 553644032 | bytes 22462468 | tf_op jit(solution)/shard_map/qcrd,kcd->crqk/dot_general | solution.py:86
  131.0 5.1 %fusion.16 = bf16[8,512,512]{1,2,0:T(8,128)(2,1)S(1)} fusion(f32[512,512,8]{1,0,2:T(8,128)} %get-tuple-element.45, bf16[1,8,512,512]{2,3,1,0:T(8,128)(2,1)S(1)} %get-tuple-element.27, f32[8,512]{1,0:T(8,128)S(1)} %get-tuple-element.26), kind=kLoop, calls=%fused_computation.24 | loop fusion | flops 10485760 | bytes 16793600 | tf_op jit(solution)/shard_map/reshape.36
  136.2 1.9 copy-done.1
  141.6 26.9 %all-gather.2.cloned.1.call-done = bf16[512,2,4,128]{3,0,2,1:T(8,128)(2,1)} async-done(((bf16[512,2,1,128]{3,0,2,1:T(8,128)(2,1)}), bf16[512,2,4,128]{3,0,2,1:T(8,128)(2,1)}) %all-gather.2.cloned.1.call-update) | async-done | bytes 1048592 | tf_op jit(solution)/shard_map/all_gather | solution.py:98
  170.0 4.4 %convolution_convert_fusion.1 = bf16[2048,512]{1,0:T(8,128)(2,1)} fusion(bf16[512,2,512]{0,2,1:T(8,128)(2,1)S(1)} %bitcast.144, bf16[512,2048]{1,0:T(8,128)(2,1)} %param.7, f32[2048]{0:T(1024)S(1)} %copy-done.11, f32[512]{0:T(512)S(1)} %add_rsqrt_fusion), kind=kOutput, calls=%fused_computation.31 | convolution fusion | flops 1078984704 | bytes 4728832 | tf_op jit(solution)/shard_map/dot_general | solution.py:108
  174.5 4.4 %convolution_convert_fusion = bf16[2048,512]{1,0:T(8,128)(2,1)} fusion(bf16[512,2,512]{0,2,1:T(8,128)(2,1)S(1)} %bitcast.145, bf16[512,2048]{1,0:T(8,128)(2,1)} %param.7, f32[2048]{0:T(1024)S(1)} %copy-done.11, f32[512]{0:T(512)S(1)} %add_rsqrt_fusion), kind=kOutput, calls=%fused_computation.30 | convolution fusion | flops 1078984704 | bytes 4728832 | tf_op jit(solution)/shard_map/dot_general | solution.py:109
  179.0 4.3 %convolution_bitcast_fusion = f32[512,1,8,128]{3,0,2,1:T(8,128)S(1)} fusion(bf16[8,512,512]{1,2,0:T(8,128)(2,1)} %copy-done.1, bf16[512,64]{1,0:T(8,128)(2,1)} %get-tuple-element.39, bf16[512,64]{1,0:T(8,128)(2,1)S(1)} %get-tuple-element.38), kind=kOutput, calls=%fused_computation.37 | convolution fusion | flops 537133056 | bytes 6422528 | tf_op jit(solution)/shard_map/crqk,kcd->qcrd/dot_general | solution.py:92
  184.1 1.5 pad_maximum_fusion.2
  185.7 2.3 copy.63
  187.9 2.3 copy.65
  190.2 4.0 %fusion.21 = bf16[128,8,512]{2,0,1:T(8,128)(2,1)} fusion(bf16[1,8,512,512]{2,3,1,0:T(8,128)(2,1)} %copy-done.4, bf16[512,1,4,128]{0,3,2,1:T(8,128)(2,1)} %get-tuple-element.33, s32[]{:T(128)S(6)} %select_n.18), kind=kOutput, calls=%fused_computation.38 | convolution fusion | flops 537395200 | bytes 5373956 | tf_op jit(solution)/shard_map/crqk,kcd->qcrd/dot_general | solution.py:81
  194.2 2.3 copy.64
  197.7 3.1 %fusion.41 = f32[512,2048]{1,0:T(8,128)S(1)} fusion(bf16[2048,512]{1,0:T(8,128)(2,1)} %param.9, bf16[512,2,512]{0,2,1:T(8,128)(2,1)S(1)} %bitcast.146), kind=kOutput, calls=%fused_computation.60 | convolution fusion | flops 1073741824 | bytes 6815744 | tf_op jit(solution)/shard_map/dot_general | solution.py:105
  200.8 4.1 %fusion.14 = (bf16[2048]{0:T(1024)(128)(2,1)S(1)}, f32[512]{0:T(512)S(1)}, f32[512,2048]{1,0:T(8,128)}) fusion(bf16[512,2048]{1,0:T(8,128)(2,1)S(1)} %copy-done.3, f32[512]{0:T(512)S(1)} %add_rsqrt_fusion, f32[2048]{0:T(1024)S(1)} %copy-done.11, f32[512,2048]{1,0:T(8,128)S(1)} %fusion.41, bf16[2048,512]{1,0:T(8,128)(2,1)S(1)} %copy-done, ...), kind=kOutput, calls=%fused_computation.22 | convolution fusion | flops 1082127872 | bytes 13123584 | tf_op jit(solution)/shard_map/dot_general | solution.py:105
  204.9 8.9 %psum.23 = f32[512]{0:T(512)S(1)} all-reduce(f32[512]{0:T(512)S(1)} %get-tuple-element.25), channel_id=1, replica_groups=mesh['dp'=8,'tensor'=4] {'tensor'}, use_global_device_ids=true, to_apply=%region_8.9 | all-reduce | flops 512 | bytes 4096 | tf_op jit(solution)/shard_map/psum | solution.py:123
  213.8 14.4 %all-reduce = bf16[2048]{0:T(1024)(128)(2,1)S(1)} all-reduce(bf16[2048]{0:T(1024)(128)(2,1)S(1)} %get-tuple-element.24), channel_id=4, replica_groups=mesh['dp'=8,'tensor'=4] {'dp'}, use_global_device_ids=true, to_apply=%region_12.13.clone | all-reduce | flops 2048 | bytes 8192
  228.8 5.2 %fusion.13 = bf16[512,2048]{1,0:T(8,128)(2,1)} fusion(bf16[512,2048]{1,0:T(8,128)(2,1)} %param.7, f32[512,2048]{1,0:T(8,128)} %get-tuple-element.46, f32[512]{0:T(512)S(1)} %broadcast_multiply_fusion.1, f32[2048]{0:T(1024)S(1)} %copy-done.11, f32[512]{0:T(512)S(1)} %add_rsqrt_fusion), kind=kLoop, calls=%fused_computation.21 | loop fusion | flops 7340032 | bytes 8400896 | tf_op jit(solution)/shard_map/convert_element_type | solution.py:124
  234.0 1.8 convert_element_type.146
  235.8 11.2 %reduce-scatter.5.cloned.1.call-done = bf16[256,512]{1,0:T(8,128)(2,1)} async-done(((bf16[2048,512]{1,0:T(8,128)(2,1)}), bf16[256,512]{1,0:T(8,128)(2,1)}) %reduce-scatter.5.cloned.1.call-update) | async-done | bytes 262160 | tf_op jit(solution)/shard_map/reduce_scatter | solution.py:115
  247.0 1.8 convert_element_type.148
  (60 shorter events, 17.0 us)
Async XLA Ops:
  7.2 15.6 %copy-start = (bf16[2048,512]{1,0:T(8,128)(2,1)S(1)}, bf16[2048,512]{1,0:T(8,128)(2,1)}, u32[]{:S(2)}) copy-start(bf16[2048,512]{1,0:T(8,128)(2,1)} %param.10) | copy-start | bytes 6291460
  7.2 161.4 %all-gather.2.cloned.1.call-start = ((), (), s32[]{:S(2)}) async-start(), calls=%async_computation.2 | async-start | bytes 1310720 | tf_op jit(solution)/shard_map/all_gather | solution.py:98
  7.2 95.6 %copy-start.12 = (f32[64]{0:T(128)}, f32[64]{0:T(128)S(1)}, u32[]{:S(2)}) copy-start(f32[64]{0:T(128)S(1)} %negate_power_fusion) | copy-start | bytes 772
  22.7 3.2 %copy-start.2 = (bf16[512,2048]{1,0:T(8,128)(2,1)S(1)}, bf16[512,2048]{1,0:T(8,128)(2,1)}, u32[]{:S(2)}) copy-start(bf16[512,2048]{1,0:T(8,128)(2,1)} %param.7) | copy-start | bytes 6291460
  22.7 3.2 %copy-start.7 = (bf16[2048,512]{1,0:T(8,128)(2,1)S(1)}, bf16[2048,512]{1,0:T(8,128)(2,1)}, u32[]{:S(2)}) copy-start(bf16[2048,512]{1,0:T(8,128)(2,1)} %param.9) | copy-start | bytes 6291460
  22.8 3.2 %copy-start.11 = (f32[2048]{0:T(1024)S(1)}, f32[2048]{0:T(1024)}, u32[]{:S(2)}) copy-start(f32[2048]{0:T(1024)} %param.8) | copy-start | bytes 24580
  110.3 6.4 %copy-start.5 = (f32[512,64]{1,0:T(8,128)S(1)}, f32[512,64]{1,0:T(8,128)}, u32[]{:S(2)}) copy-start(f32[512,64]{1,0:T(8,128)} %get-tuple-element.42) | copy-start | bytes 393220
  110.3 6.4 %copy-start.10 = (f32[512,64]{1,0:T(8,128)S(1)}, f32[512,64]{1,0:T(8,128)}, u32[]{:S(2)}) copy-start(f32[512,64]{1,0:T(8,128)} %get-tuple-element.41) | copy-start | bytes 393220
  116.7 2.8 %copy-start.8 = (bf16[512,64]{1,0:T(8,128)(2,1)S(1)}, bf16[512,64]{1,0:T(8,128)(2,1)}, u32[]{:S(2)}) copy-start(bf16[512,64]{1,0:T(8,128)(2,1)} %get-tuple-element.39) | copy-start | bytes 196612
  121.8 1.8 copy-start.14
  129.8 6.4 %copy-start.4 = (bf16[1,8,512,512]{2,3,1,0:T(8,128)(2,1)}, bf16[1,8,512,512]{2,3,1,0:T(8,128)(2,1)S(1)}, u32[]{:S(2)}) copy-start(bf16[1,8,512,512]{2,3,1,0:T(8,128)(2,1)S(1)} %get-tuple-element.27) | copy-start | bytes 12582916
  136.2 1.9 copy-start.1
  138.1 1.3 copy-start.13
  141.6 92.4 %reduce-scatter.3.cloned.1.call-start = ((), (), s32[]{:S(2)}) async-start(), calls=%async_computation.3 | async-start | bytes 2359296 | tf_op jit(solution)/shard_map/reduce_scatter | solution.py:112
  174.5 72.6 %reduce-scatter.5.cloned.1.call-start = ((), (), s32[]{:S(2)}) async-start(), calls=%async_computation.4 | async-start | bytes 2359296 | tf_op jit(solution)/shard_map/reduce_scatter | solution.py:115
  178.9 4.4 %copy-start.6 = (f32[512,64]{1,0:T(8,128)S(1)}, f32[512,64]{1,0:T(8,128)}, u32[]{:S(2)}) copy-start(f32[512,64]{1,0:T(8,128)} %get-tuple-element.42) | copy-start | bytes 393220
  179.0 4.4 %copy-start.9 = (f32[512,64]{1,0:T(8,128)S(1)}, f32[512,64]{1,0:T(8,128)}, u32[]{:S(2)}) copy-start(f32[512,64]{1,0:T(8,128)} %get-tuple-element.40) | copy-start | bytes 393220
  190.2 6.3 %copy-start.15 = (u32[32]{0:T(128)S(1)}, u32[32]{0:T(128)}, u32[]{:S(2)}) copy-start(u32[32]{0:T(128)} %constant.57) | copy-start | bytes 388
  197.7 3.1 %copy-start.3 = (bf16[512,2048]{1,0:T(8,128)(2,1)S(1)}, bf16[512,2048]{1,0:T(8,128)(2,1)}, u32[]{:S(2)}) copy-start(bf16[512,2048]{1,0:T(8,128)(2,1)} %param.7) | copy-start | bytes 6291460
Sparse Core Ops, SparseCore 0:
  141.7 26.8 all-gather.1
  174.6 35.7 reduce-scatter.2
  212.7 34.3 reduce-scatter.4
where the time goes:
time: 256 us; the launch traced here: 255 us
  blocking collectives  106 us (41%)
  matrix products  39.9 us (16%)
  waiting for transfers between devices  38.2 us (15%)
  other arithmetic  33.5 us (13%)
  local copies, waits for them, and re-layouts  22.5 us (9%)
  between operations  14.7 us (6%)
    psum x1, blocking collectives, body(): lax.psum(partial_value.reshape(rows, 2 * width), 'tensor')  71.8 us
    all_gather x1, waiting for transfers between devices, body(): lax.all_gather(grad_part.astype(jnp.bfloat16), 'tensor', axis=2, tiled=True)  26.9 us
    unnamed x39, local copies, waits for them, and re-layouts  15.1 us
    unnamed x1, blocking collectives  14.4 us
    psum x1, blocking collectives, body(): square_sum = lax.psum(jnp.sum(in_float * in_float, axis=1), 'tensor')  11.4 us
    reduce_scatter x1, waiting for transfers between devices, body(): lax.psum_scatter(value_term.astype(jnp.bfloat16), 'dp', scatter_dimension...  11.2 us
    psum x1, blocking collectives, body(): corr = lax.psum(jnp.sum(d_unit * unit, axis=1), 'tensor') / D  8.87 us
    another operation x3, other arithmetic  7.13 us
  transfers between devices with their start and end apart: 3, of which 2 were waited for; matrix products, arithmetic and copies ran while one was open for 15% of the time, Pallas kernels for 0%

commit v1 on v0

--- a/solution.py
+++ b/solution.py
@@ -1,6 +1,11 @@
+import functools
+
 import jax
 import jax.numpy as jnp
+import numpy as np
 from jax import lax
+from jax.experimental import pallas as pl
+from jax.experimental.pallas import tpu as pltpu
 from jax.sharding import PartitionSpec as P
 
 D = 8192
@@ -40,7 +45,7 @@
     return (pos, allowed)
 
 
-def body(hidden_in, norm_gain, key_weight, value_weight, queries, segments, cotangent):
+def plain_body(hidden_in, norm_gain, key_weight, value_weight, queries, segments, cotangent):
     rows = hidden_in.shape[0]
     width = key_weight.shape[1]
     group = HQ // KVH
@@ -125,7 +130,497 @@
     return (attn_out, grad_hidden, grad_queries, grad_key, grad_value, grad_gain)
 
 
+ZS = 4
+TS = 4
+ROWS = 512
+FEAT = 2048
+BLK = 128
+NB = ROWS // BLK
+HEADS = HQ // TS
+GH = 4
+KV = 2 * HD
+SH = FEAT // (2 * ZS)
+KV_SEND = jnp.float32
+MESH = pl.DeviceIdType.MESH
+F32 = jnp.float32
+BF16 = jnp.bfloat16
+
+
+def dot_nn(a, b):
+    return lax.dot_general(a, b, (((1,), (0,)), ((), ())), preferred_element_type=F32)
+
+
+def dot_nt(a, b):
+    return lax.dot_general(a, b, (((1,), (1,)), ((), ())), preferred_element_type=F32)
+
+
+def dot_tn(a, b):
+    return lax.dot_general(a, b, (((0,), (0,)), ((), ())), preferred_element_type=F32)
+
+
+def eye_mask():
+    return lax.broadcasted_iota(jnp.int32, (BLK, BLK), 0) == lax.broadcasted_iota(
+        jnp.int32, (BLK, BLK), 1
+    )
+
+
+def col_to_row(col):
+    return jnp.sum(jnp.where(eye_mask(), col, 0.0), axis=0, keepdims=True)
+
+
+def row_to_col(row):
+    return jnp.sum(jnp.where(eye_mask(), row, 0.0), axis=1, keepdims=True)
+
+
+def swap_halves(vec):
+    return pltpu.roll(vec, HD // 2, vec.ndim - 1)
+
+
+def fused_kernel(
+    hid_h, gain_v, kw_h, vw_h, q_h, seg_v, cot_h, freq_v,
+    ao_h, gh_h, gq_h, gk_h, gv_h, gg_v,
+    hid, w4, qs, cs, qr, cosv, sinv, segc, invc, normed, nt,
+    ss, sbuf, rbuf, own_kv, krot, vals, dk_acc, dv_acc, ao, gq,
+    dkv, du, corr_acc, cc, gsend, grecv,
+    csend, crecv, own, zsend, zfl, zfr, gkv, gvv, gh,
+    in_sem, out_sem, ss_s, ss_r, kv_s, kv_r, ag_s, ag_r, co_s, co_r,
+    ga_s, ga_r, cx_s, cx_r, zs_s, zl_r, zr_r,
+):
+    dp = lax.axis_index("dp")
+    t = lax.axis_index("tensor")
+    z = dp // 2
+    core = dp % 2
+    other = 1 - core
+    dp_other = dp + 1 - 2 * core
+    peers = [t, t + 1 - 2 * (t % 2), (t + 2) % 4, 3 - t]
+
+    def remote(src, dst, ssem, rsem, dev):
+        return pltpu.make_async_remote_copy(
+            src_ref=src, dst_ref=dst, send_sem=ssem, recv_sem=rsem,
+            device_id=dev, device_id_type=MESH,
+        )
+
+    barrier = pltpu.get_barrier_semaphore()
+    for p in range(1, 4):
+        pl.semaphore_signal(barrier, inc=1, device_id=(dp, peers[p]), device_id_type=MESH)
+    for k in range(1, 2 * ZS):
+        pl.semaphore_signal(
+            barrier, inc=1, device_id=((dp + k) % (2 * ZS), t), device_id_type=MESH
+        )
+
+    loads = [pltpu.make_async_copy(hid_h, hid, in_sem.at[0])]
+    q_loads = [
+        pltpu.make_async_copy(q_h.at[:, pl.ds(h * HD, HD)], qs.at[h], in_sem.at[1 + h])
+        for h in range(HEADS)
+    ]
+    w_loads = []
+    for h in range(KVH):
+        w_loads.append(pltpu.make_async_copy(
+            kw_h.at[:, pl.ds(h * HD, HD)], w4.at[h, :, pl.ds(0, HD)], in_sem.at[9 + 2 * h]))
+        w_loads.append(pltpu.make_async_copy(
+            vw_h.at[:, pl.ds(h * HD, HD)], w4.at[h, :, pl.ds(HD, HD)], in_sem.at[10 + 2 * h]))
+    c_loads = [
+        pltpu.make_async_copy(cot_h.at[:, pl.ds(h * HD, HD)], cs.at[h], in_sem.at[17 + h])
+        for h in range(HEADS)
+    ]
+    for c in loads + q_loads + w_loads + c_loads:
+        c.start()
+
+    loads[0].wait()
+    for b in range(NB):
+        x = hid[pl.ds(b * BLK, BLK), :].astype(F32)
+        ss[0, :, pl.ds(b * BLK, BLK)] = jnp.broadcast_to(
+            col_to_row(jnp.sum(x * x, axis=1, keepdims=True)), (8, BLK)
+        )
+    pl.semaphore_wait(barrier, 3 + 2 * ZS - 1)
+
+    def ss_copy(p):
+        return remote(ss.at[0], ss.at[p], ss_s.at[p - 1], ss_r.at[p - 1], (dp, peers[p]))
+
+    for p in range(1, 4):
+        ss_copy(p).start()
+
+    segr = seg_v[...].astype(F32)
+    for b in range(NB):
+        rows = pl.ds(b * BLK, BLK)
+        col = row_to_col(segr[:, b * BLK:(b + 1) * BLK])
+        segc[rows, :] = col
+        start = jnp.sum(jnp.where(segr < col, 1.0, 0.0), axis=1, keepdims=True)
+        index = lax.broadcasted_iota(jnp.int32, (BLK, 1), 0).astype(F32) + float(b * BLK)
+        angle = (index - start) * freq_v[...]
+        lane = lax.broadcasted_iota(jnp.int32, (BLK, HD), 1)
+        cosv[rows, :] = jnp.cos(angle)
+        sinv[rows, :] = jnp.where(lane < HD // 2, -1.0, 1.0) * jnp.sin(angle)
+    for c in q_loads:
+        c.wait()
+
+    def rot_query(h, carry):
+        v = qs[h].astype(F32)
+        qr[h] = (v * cosv[...] + swap_halves(v) * sinv[...]).astype(BF16)
+        return carry
+
+    lax.fori_loop(0, HEADS, rot_query, 0)
+
+    for p in range(1, 4):
+        ss_copy(p).wait_recv()
+    total = ss[0, 0:1, :] + ss[1, 0:1, :] + ss[2, 0:1, :] + ss[3, 0:1, :]
+    inv_row = lax.rsqrt(total / D + 1e-05)
+    for b in range(NB):
+        invc[pl.ds(b * BLK, BLK), :] = row_to_col(inv_row[:, b * BLK:(b + 1) * BLK])
+    for c in w_loads:
+        c.wait()
+
+    def kv_copy(b, p):
+        return remote(
+            sbuf.at[b, p - 1], rbuf.at[b, p - 1], kv_s.at[b, p - 1], kv_r.at[b, p - 1],
+            (dp, peers[p]),
+        )
+
+    for b in range(NB):
+        rows = pl.ds(b * BLK, BLK)
+        unit = hid[rows, :].astype(F32) * invc[rows, :]
+        normed[rows, :] = (unit * gain_v[...]).astype(BF16)
+        for p in (3, 1, 2, 0):
+            part = dot_nn(normed[rows, :], w4[peers[p]])
+            if p == 0:
+                own_kv[b] = part
+            else:
+                sbuf[b, p - 1] = part.astype(KV_SEND)
+                kv_copy(b, p).start()
+    for b in range(NB):
+        rows = pl.ds(b * BLK, BLK)
+        nt[:, pl.ds(b * BLK, BLK)] = normed[rows, :].astype(F32).T.astype(BF16)
+    for c in c_loads:
+        c.wait()
+
+    dk_acc[...] = jnp.zeros_like(dk_acc)
+    dv_acc[...] = jnp.zeros_like(dv_acc)
+    scale = 1.0 / HD**0.5
+
+    def ag_copy(part, p):
+        rows = pl.ds(0, BLK) if part == 0 else pl.ds(BLK, ROWS - BLK)
+        return remote(
+            dkv.at[t, rows], dkv.at[t, rows], ag_s.at[part, p - 1], ag_r.at[part, p - 1],
+            (dp, peers[p]),
+        )
+
+    def ag_wait(part, p):
+        rows = pl.ds(0, BLK) if part == 0 else pl.ds(BLK, ROWS - BLK)
+        remote(
+            dkv.at[peers[p], rows], dkv.at[peers[p], rows], ag_s.at[part, p - 1],
+            ag_r.at[part, p - 1], (dp, peers[p]),
+        ).wait_recv()
+
+    def finish_grads(part):
+        rows = pl.ds(0, BLK) if part == 0 else pl.ds(BLK, ROWS - BLK)
+        dk = dk_acc[rows, :]
+        dkv[t, rows, pl.ds(0, HD)] = (
+            dk * cosv[rows, :] - swap_halves(dk) * sinv[rows, :]
+        ).astype(BF16)
+        dkv[t, rows, pl.ds(HD, HD)] = dv_acc[rows, :].astype(BF16)
+        for p in (3, 1, 2):
+            ag_copy(part, p).start()
+
+    for b in range(NB):
+        rows = pl.ds(b * BLK, BLK)
+        low = max(0, b - 2) * BLK
+        width = (b + 1) * BLK - low
+        window = pl.ds(low, width)
+        for p in range(1, 4):
+            kv_copy(b, p).wait_recv()
+        both = own_kv[b]
+        for p in range(1, 4):
+            both = both + rbuf[b, p - 1].astype(F32)
+        both = both.astype(BF16)
+        key = both[:, :HD].astype(F32)
+        krot[rows, :] = (key * cosv[rows, :] + swap_halves(key) * sinv[rows, :]).astype(BF16)
+        vals[rows, :] = both[:, HD:]
+        q_index = lax.broadcasted_iota(jnp.int32, (BLK, width), 0) + b * BLK
+        k_index = lax.broadcasted_iota(jnp.int32, (BLK, width), 1) + low
+        same = segc[rows, :] == segr[:, low:low + width]
+        bias = jnp.where(same & (k_index <= q_index), 0.0, -1e30)
+
+        def group(g, carry):
+            heads = pl.ds(g * GH, GH)
+            qg = qr[heads, rows, :].reshape(GH * BLK, HD)
+            cg = cs[heads, rows, :].reshape(GH * BLK, HD)
+            kwin = krot[window, :]
+            vwin = vals[window, :]
+            s = dot_nt(qg, kwin).reshape(GH, BLK, width) * scale + bias[None]
+            e = jnp.exp(s - jnp.max(s, axis=-1, keepdims=True))
+            pb = (e * (1.0 / jnp.sum(e, axis=-1, keepdims=True))).astype(BF16)
+            pf = pb.astype(F32)
+            pb = pb.reshape(GH * BLK, width)
+            ao[heads, rows, :] = dot_nn(pb, vwin).astype(BF16).reshape(GH, BLK, HD)
+            dpr = dot_nt(cg, vwin).reshape(GH, BLK, width)
+            delta = jnp.sum(pf * dpr, axis=-1, keepdims=True)
+            ds = (pf * (dpr - delta) * scale).astype(BF16).reshape(GH * BLK, width)
+            dq = dot_nn(ds, kwin).reshape(GH, BLK, HD)
+            gq[heads, rows, :] = (
+                dq * cosv[rows, :][None] - swap_halves(dq) * sinv[rows, :][None]
+            ).astype(BF16)
+            dk_acc[window, :] += dot_tn(ds, qg)
+            dv_acc[window, :] += dot_tn(pb, cg)
+            return carry
+
+        lax.fori_loop(0, HEADS // GH, group, 0)
+        if b == 2:
+            finish_grads(0)
+    finish_grads(1)
+
+    outs = []
+    for h in range(HEADS):
+        outs.append(pltpu.make_async_copy(ao.at[h], ao_h.at[:, pl.ds(h * HD, HD)], out_sem.at[h]))
+        outs.append(pltpu.make_async_copy(
+            gq.at[h], gq_h.at[:, pl.ds(h * HD, HD)], out_sem.at[HEADS + h]))
+    for c in outs:
+        c.start()
+
+    def cx_copy(p, zt):
+        return remote(
+            csend.at[p, zt], crecv.at[p, zt], cx_s.at[p, zt], cx_r.at[p, zt], (dp_other, t)
+        )
+
+    def partials(p):
+        for zt in range(ZS):
+            far = nt[pl.ds((2 * zt + other) * SH, SH), :]
+            csend[p, zt] = dot_nn(far, dkv[peers[p]]).astype(BF16)
+            cx_copy(p, zt).start()
+        for zt in range(ZS):
+            near = nt[pl.ds((2 * zt + core) * SH, SH), :]
+            own[p, zt] = dot_nn(near, dkv[peers[p]])
+
+    def pair_sums(p):
+        for zt in (3, 0, 2, 1):
+            cx_copy(p, zt).wait_recv()
+            own[p, zt] = own[p, zt] + crecv[p, zt].astype(F32)
+
+    def right_copy(p, zt):
+        return remote(
+            zsend.at[p, zt], zfl.at[p, zt], zs_s.at[p, zt], zl_r.at[p, zt], ((dp + 2) % (2 * ZS), t)
+        )
+
+    def left_copy(p, zt):
+        return remote(
+            zsend.at[p, zt], zfr.at[p, zt], zs_s.at[p, zt], zr_r.at[p, zt], ((dp + 2 * ZS - 2) % (2 * ZS), t)
+        )
+
+    def end_sends(p):
+        @pl.when(z == 0)
+        def _():
+            for zt in range(ZS - 1, 0, -1):
+                zsend[p, zt] = own[p, zt].astype(BF16)
+                right_copy(p, zt).start()
+
+        @pl.when(z == ZS - 1)
+        def _():
+            for zt in range(ZS - 1):
+                zsend[p, zt] = own[p, zt].astype(BF16)
+                left_copy(p, zt).start()
+
+    def middle_sends(p):
+        for k in range(ZS - 1):
+            zt = ZS - 1 - k
+
+            @pl.when((z > 0) & (z < zt))
+            def _():
+                right_copy(p, zt).wait_recv()
+                zsend[p, zt] = (own[p, zt] + zfl[p, zt].astype(F32)).astype(BF16)
+                right_copy(p, zt).start()
+
+            @pl.when((z < ZS - 1) & (z > k))
+            def _():
+                left_copy(p, k).wait_recv()
+                zsend[p, k] = (own[p, k] + zfr[p, k].astype(F32)).astype(BF16)
+                left_copy(p, k).start()
+
+    partials(0)
+    pair_sums(0)
+    end_sends(0)
+    for p in range(1, 4):
+        ag_wait(0, p)
+        ag_wait(1, p)
+        partials(p)
+    for p in range(1, 4):
+        pair_sums(p)
+        end_sends(p)
+
+    corr_acc[...] = jnp.zeros_like(corr_acc)
+
+    def feature_chunk(f, carry):
+        cols = pl.ds(pl.multiple_of(f * SH, SH), SH)
+        dn = dot_nt(dkv[0], w4[0, cols, :])
+        for h in range(1, KVH):
+            dn = dn + dot_nt(dkv[h], w4[h, cols, :])
+        unit = hid[:, cols].astype(F32) * invc[...]
+        gsend[f] = jnp.sum((dn * unit).reshape(ROWS // 8, 8, SH), axis=0)
+        dun = dn * gain_v[:, cols]
+        du[:, cols] = dun
+        w = dun * unit
+        corr_acc[...] += w[:, :128] + w[:, 128:]
+        return carry
+
+    lax.fori_loop(0, 2 * ZS, feature_chunk, 0)
+    for b in range(NB):
+        rows = pl.ds(b * BLK, BLK)
+        cc[0, :, rows] = jnp.broadcast_to(
+            col_to_row(jnp.sum(corr_acc[rows, :], axis=1, keepdims=True)), (8, BLK)
+        )
+
+    def cc_copy(p):
+        return remote(cc.at[0], cc.at[p], co_s.at[p - 1], co_r.at[p - 1], (dp, peers[p]))
+
+    def gain_copy(k):
+        to = (dp + k) % (2 * ZS)
+        return remote(gsend.at[to], grecv.at[k], ga_s.at[k], ga_r.at[k], (to, t))
+
+    for p in range(1, 4):
+        cc_copy(p).start()
+    for k in range(1, 2 * ZS):
+        gain_copy(k).start()
+
+    middle_sends(0)
+    for p in range(1, 4):
+        cc_copy(p).wait_recv()
+    corr_row = (cc[0, 0:1, :] + cc[1, 0:1, :] + cc[2, 0:1, :] + cc[3, 0:1, :]) / D
+    for b in range(NB):
+        rows = pl.ds(b * BLK, BLK)
+        corr = row_to_col(corr_row[:, b * BLK:(b + 1) * BLK])
+        inv = invc[rows, :]
+        unit = hid[rows, :].astype(F32) * inv
+        gh[rows, :] = (inv * (du[rows, :] - unit * corr)).astype(BF16)
+    gh_out = pltpu.make_async_copy(gh, gh_h, out_sem.at[2 * HEADS])
+    gh_out.start()
+
+    for p in range(1, 4):
+        middle_sends(p)
+
+    for k in range(1, 2 * ZS):
+        gain_copy(k).wait_recv()
+    gain_sum = gsend[dp]
+    for k in range(1, 2 * ZS):
+        gain_sum = gain_sum + grecv[k]
+    gg_v[...] = jnp.sum(gain_sum, axis=0, keepdims=True)
+
+    for p in range(4):
+        for zt in range(ZS):
+            @pl.when(z == zt)
+            def _():
+                res = own[p, zt]
+                if zt > 0:
+                    right_copy(p, zt).wait_recv()
+                    res = res + zfl[p, zt].astype(F32)
+                if zt < ZS - 1:
+                    left_copy(p, zt).wait_recv()
+                    res = res + zfr[p, zt].astype(F32)
+                cols = pl.ds(pl.multiple_of(peers[p] * HD, HD), HD)
+                gkv[:, cols] = res[:, :HD]
+                gvv[:, cols] = res[:, HD:]
+    gk_out = pltpu.make_async_copy(gkv, gk_h, out_sem.at[2 * HEADS + 1])
+    gv_out = pltpu.make_async_copy(gvv, gv_h, out_sem.at[2 * HEADS + 2])
+    gk_out.start()
+    gv_out.start()
+
+    for p in range(1, 4):
+        ss_copy(p).wait_send()
+        cc_copy(p).wait_send()
+        ag_copy(0, p).wait_send()
+        ag_copy(1, p).wait_send()
+        for b in range(NB):
+            kv_copy(b, p).wait_send()
+    for k in range(1, 2 * ZS):
+        gain_copy(k).wait_send()
+    for p in range(4):
+        for zt in range(ZS):
+            cx_copy(p, zt).wait_send()
+
+            @pl.when(z != zt)
+            def _():
+                right_copy(p, zt).wait_send()
+    for c in outs + [gh_out, gk_out, gv_out]:
+        c.wait()
+
+
+def fused_body(hidden_in, norm_gain, key_weight, value_weight, queries, segments, cotangent):
+    half = np.arange(HD // 2, dtype=np.float32) * np.float32(2.0 / HD)
+    freq = np.power(np.float32(ROPE_BASE), -half).astype(np.float32)
+    freq = jnp.asarray(np.concatenate([freq, freq])[None, :])
+    vmem = pl.BlockSpec(memory_space=pltpu.VMEM)
+    hbm = pl.BlockSpec(memory_space=pl.ANY)
+    dma = pltpu.SemaphoreType.DMA
+    V = pltpu.VMEM
+    outs = pl.pallas_call(
+        fused_kernel,
+        out_shape=(
+            jax.ShapeDtypeStruct((ROWS, HEADS * HD), BF16),
+            jax.ShapeDtypeStruct((ROWS, FEAT), BF16),
+            jax.ShapeDtypeStruct((ROWS, HEADS * HD), BF16),
+            jax.ShapeDtypeStruct((SH, KVH * HD), F32),
+            jax.ShapeDtypeStruct((SH, KVH * HD), F32),
+            jax.ShapeDtypeStruct((1, SH), F32),
+        ),
+        in_specs=[hbm, vmem, hbm, hbm, hbm, vmem, hbm, vmem],
+        out_specs=(hbm, hbm, hbm, hbm, hbm, vmem),
+        scratch_shapes=[
+            V((ROWS, FEAT), BF16),
+            V((KVH, FEAT, KV), BF16),
+            V((HEADS, ROWS, HD), BF16),
+            V((HEADS, ROWS, HD), BF16),
+            V((HEADS, ROWS, HD), BF16),
+            V((ROWS, HD), F32),
+            V((ROWS, HD), F32),
+            V((ROWS, 1), F32),
+            V((ROWS, 1), F32),
+            V((ROWS, FEAT), BF16),
+            V((FEAT, ROWS), BF16),
+            V((4, 8, ROWS), F32),
+            V((NB, 3, BLK, KV), KV_SEND),
+            V((NB, 3, BLK, KV), KV_SEND),
+            V((NB, BLK, KV), F32),
+            V((ROWS, HD), BF16),
+            V((ROWS, HD), BF16),
+            V((ROWS, HD), F32),
+            V((ROWS, HD), F32),
+            V((HEADS, ROWS, HD), BF16),
+            V((HEADS, ROWS, HD), BF16),
+            V((KVH, ROWS, KV), BF16),
+            V((ROWS, FEAT), F32),
+            V((ROWS, 128), F32),
+            V((4, 8, ROWS), F32),
+            V((2 * ZS, 8, SH), F32),
+            V((2 * ZS, 8, SH), F32),
+            V((4, ZS, SH, KV), BF16),
+            V((4, ZS, SH, KV), BF16),
+            V((4, ZS, SH, KV), F32),
+            V((4, ZS, SH, KV), BF16),
+            V((4, ZS, SH, KV), BF16),
+            V((4, ZS, SH, KV), BF16),
+            V((SH, KVH * HD), F32),
+            V((SH, KVH * HD), F32),
+            V((ROWS, FEAT), BF16),
+            dma((25,)), dma((2 * HEADS + 3,)),
+            dma((3,)), dma((3,)),
+            dma((NB, 3)), dma((NB, 3)),
+            dma((2, 3)), dma((2, 3)),
+            dma((3,)), dma((3,)),
+            dma((2 * ZS,)), dma((2 * ZS,)),
+            dma((4, ZS)), dma((4, ZS)),
+            dma((4, ZS)), dma((4, ZS)), dma((4, ZS)),
+        ],
+        compiler_params=pltpu.CompilerParams(
+            collective_id=0, has_side_effects=True, vmem_limit_bytes=56 * 1024 * 1024
+        ),
+        name="fused_block",
+    )(
+        hidden_in, norm_gain[None, :], key_weight, value_weight, queries, segments, cotangent,
+        freq,
+    )
+    return outs[:5] + (outs[5][0],)
+
+
 def solution(mesh):
+    fused = (mesh.shape["dp"], mesh.shape["tensor"]) == (2 * ZS, TS)
+    body = fused_body if fused else plain_body
     return jax.shard_map(
         body,
         mesh=mesh,

time: 256 us -> 114 us (0.45)
  Pallas kernels: 0 us -> 106 us
  blocking collectives: 106 us -> 0 us
  matrix products: 39.9 us -> 0 us
  waiting for transfers between devices: 38.2 us -> 0 us
  other arithmetic: 33.5 us -> 0 us
  local copies, waits for them, and re-layouts: 22.5 us -> 7.9 us
  between operations: 14.7 us -> 0.66 us
    pallas_call x0 -> x1, Pallas kernels: none -> 106 us  [fused_body(): pl.pallas_call(fused_kernel, out_shape=(jax.ShapeDtypeStruct((ROWS, HEADS...]
    psum x3 -> x0, blocking collectives: 92 us -> none  [the longest x1 71.8 us: body(): lax.psum(partial_value.reshape(rows, 2 * width), 'tensor')]
    dot_general x12 -> x0, matrix products: 39.9 us -> none  [the longest x1 6.17 us: body(): jnp.einsum('qcrd,kcd->crqk', cot_four, value_local, preferred_element_typ...]
    all_gather x1 -> x0, waiting for transfers between devices: 26.9 us -> none  [body(): lax.all_gather(grad_part.astype(jnp.bfloat16), 'tensor', axis=2, tiled=True)]
    unnamed x1 -> x0, blocking collectives: 14.4 us -> none
    reduce_scatter x2 -> x0, waiting for transfers between devices: 11.2 us -> none  [the longest x1 11.2 us: body(): lax.psum_scatter(value_term.astype(jnp.bfloat16), 'dp', scatter_dimension...]
    another operation x6 -> x0, other arithmetic: 9.46 us -> none
    convert_element_type x6 -> x0, other arithmetic: 9.44 us -> none  [the longest x1 5.16 us: body(): (inv_rms[:, None] * (d_unit - unit * corr[:, None])).astype(jnp.bfloat16)]
  transfers between devices with their start and end apart: 3 -> 0, of which waited for: 2 -> 0; matrix products, arithmetic and copies ran while one was open for 15% -> 0% of each run, Pallas kernels for 0% -> 0%
where the time goes in v1:
time: 114 us
  Pallas kernels  106 us (93%)
  local copies, waits for them, and re-layouts  7.9 us (7%)
    pallas_call x1, Pallas kernels, fused_body(): pl.pallas_call(fused_kernel, out_shape=(jax.ShapeDtypeStruct((ROWS, HEADS...  106 us
    unnamed x16, local copies, waits for them, and re-layouts  7.9 us

profile of v1, /device:TPU:0, one launch (start us, length us, event | category | flops | bytes accessed | tf_op | source)
XLA Modules:
  0.0 114.2 jit_solution(15881967470414598519)
XLA Ops:
  0.6 105.6 %fused_block.1 = (bf16[512,1024]{1,0:T(8,128)(2,1)}, bf16[512,2048]{1,0:T(8,128)(2,1)}, bf16[512,1024]{1,0:T(8,128)(2,1)}, f32[256,512]{1,0:T(8,128)}, f32[256,512]{1,0:T(8,128)}, /*index=5*/f32[1,256]{1,0:T(1,128)}) custom-call(bf16[512,2048]{1,0:T(8,128)(2,1)} %hid_h.1, f32[1,2048]{1,0:T(1,128)} %bitcast.2, bf16[2048,512]{1,0:T(8,128)(2,1)} %kw_h.1, ...), custom_call_target="tpu_custom_call" | custom-call | tf_op jit(solution)/shard_map/fused_block/pallas_call | solution.py:552
  106.3 0.0 copy-start
  106.3 2.4 %copy.20 = bf16[512,1024]{1,0:T(8,128)(2,1)} copy(bf16[512,1024]{1,0:T(8,128)(2,1)} %get-tuple-element.24) | data formatting | bytes 2097152
  108.7 0.0 copy-done
  108.7 0.0 copy-start.1
  108.7 1.3 %copy.21 = bf16[512,2048]{1,0:T(8,128)(2,1)} copy(bf16[512,2048]{1,0:T(8,128)(2,1)S(1)} %copy-done) | data formatting | bytes 4194304
  110.0 0.6 copy-done.1
  110.6 0.0 copy-start.3
  110.6 0.0 copy-start.2
  110.6 0.0 copy-start.4
  110.6 1.0 copy.22
  111.6 0.4 copy-done.3
  112.0 0.8 copy.23
  112.8 0.0 copy-done.2
  112.8 0.8 copy.24
  113.6 0.0 copy-done.4
  113.6 0.6 copy.25
Async XLA Ops:
  106.3 2.4 %copy-start = (bf16[512,2048]{1,0:T(8,128)(2,1)S(1)}, bf16[512,2048]{1,0:T(8,128)(2,1)}, u32[]{:S(2)}) copy-start(bf16[512,2048]{1,0:T(8,128)(2,1)} %get-tuple-element.25) | copy-start | bytes 6291460
  108.7 2.0 %copy-start.1 = (bf16[512,1024]{1,0:T(8,128)(2,1)S(1)}, bf16[512,1024]{1,0:T(8,128)(2,1)}, u32[]{:S(2)}) copy-start(bf16[512,1024]{1,0:T(8,128)(2,1)} %get-tuple-element.26) | copy-start | bytes 3145732
  110.6 1.4 %copy-start.3 = (f32[256,512]{1,0:T(8,128)S(1)}, f32[256,512]{1,0:T(8,128)}, u32[]{:S(2)}) copy-start(f32[256,512]{1,0:T(8,128)} %get-tuple-element.27) | copy-start | bytes 1572868
  110.6 2.2 %copy-start.2 = (f32[256,512]{1,0:T(8,128)S(1)}, f32[256,512]{1,0:T(8,128)}, u32[]{:S(2)}) copy-start(f32[256,512]{1,0:T(8,128)} %get-tuple-element.28) | copy-start | bytes 1572868
  110.6 3.0 %copy-start.4 = (f32[1,256]{1,0:T(1,128)S(1)}, f32[1,256]{1,0:T(1,128)}, u32[]{:S(2)}) copy-start(f32[1,256]{1,0:T(1,128)} %get-tuple-element.17) | copy-start | bytes 3076

commit v2 on v1

--- a/solution.py
+++ b/solution.py
@@ -140,7 +140,6 @@
 GH = 4
 KV = 2 * HD
 SH = FEAT // (2 * ZS)
-KV_SEND = jnp.float32
 MESH = pl.DeviceIdType.MESH
 F32 = jnp.float32
 BF16 = jnp.bfloat16
@@ -177,10 +176,10 @@
 
 
 def fused_kernel(
-    hid_h, gain_v, kw_h, vw_h, q_h, seg_v, cot_h, freq_v,
+    hid_h, gain_h, kw_h, vw_h, q_h, seg_h, cot_h, freq_h,
     ao_h, gh_h, gq_h, gk_h, gv_h, gg_v,
-    hid, w4, qs, cs, qr, cosv, sinv, segc, invc, normed, nt,
-    ss, sbuf, rbuf, own_kv, krot, vals, dk_acc, dv_acc, ao, gq,
+    hid, w4, qs, cs, qr, cosv, sinv, segc, invc, normed, dkvt,
+    gain_v, seg_v, freq_v, ss, ksend, vsend, krecv, vrecv, own_kv, krot, vals, dk_acc, dv_acc, ao, gq,
     dkv, du, corr_acc, cc, gsend, grecv,
     csend, crecv, own, zsend, zfl, zfr, gkv, gvv, gh,
     in_sem, out_sem, ss_s, ss_r, kv_s, kv_r, ag_s, ag_r, co_s, co_r,
@@ -223,7 +222,12 @@
         pltpu.make_async_copy(cot_h.at[:, pl.ds(h * HD, HD)], cs.at[h], in_sem.at[17 + h])
         for h in range(HEADS)
     ]
-    for c in loads + q_loads + w_loads + c_loads:
+    small = [
+        pltpu.make_async_copy(seg_h, seg_v, in_sem.at[25]),
+        pltpu.make_async_copy(freq_h, freq_v, in_sem.at[26]),
+        pltpu.make_async_copy(gain_h, gain_v, in_sem.at[27]),
+    ]
+    for c in loads + small + q_loads + w_loads + c_loads:
         c.start()
 
     loads[0].wait()
@@ -240,6 +244,8 @@
     for p in range(1, 4):
         ss_copy(p).start()
 
+    for c in small:
+        c.wait()
     segr = seg_v[...].astype(F32)
     for b in range(NB):
         rows = pl.ds(b * BLK, BLK)
@@ -251,16 +257,6 @@
         lane = lax.broadcasted_iota(jnp.int32, (BLK, HD), 1)
         cosv[rows, :] = jnp.cos(angle)
         sinv[rows, :] = jnp.where(lane < HD // 2, -1.0, 1.0) * jnp.sin(angle)
-    for c in q_loads:
-        c.wait()
-
-    def rot_query(h, carry):
-        v = qs[h].astype(F32)
-        qr[h] = (v * cosv[...] + swap_halves(v) * sinv[...]).astype(BF16)
-        return carry
-
-    lax.fori_loop(0, HEADS, rot_query, 0)
-
     for p in range(1, 4):
         ss_copy(p).wait_recv()
     total = ss[0, 0:1, :] + ss[1, 0:1, :] + ss[2, 0:1, :] + ss[3, 0:1, :]
@@ -270,9 +266,15 @@
     for c in w_loads:
         c.wait()
 
-    def kv_copy(b, p):
+    def k_copy(b, p):
         return remote(
-            sbuf.at[b, p - 1], rbuf.at[b, p - 1], kv_s.at[b, p - 1], kv_r.at[b, p - 1],
+            ksend.at[b, p - 1], krecv.at[b, p - 1], kv_s.at[0, b, p - 1], kv_r.at[0, b, p - 1],
+            (dp, peers[p]),
+        )
+
+    def v_copy(b, p):
+        return remote(
+            vsend.at[b, p - 1], vrecv.at[b, p - 1], kv_s.at[1, b, p - 1], kv_r.at[1, b, p - 1],
             (dp, peers[p]),
         )
 
@@ -285,11 +287,20 @@
             if p == 0:
                 own_kv[b] = part
             else:
-                sbuf[b, p - 1] = part.astype(KV_SEND)
-                kv_copy(b, p).start()
-    for b in range(NB):
-        rows = pl.ds(b * BLK, BLK)
-        nt[:, pl.ds(b * BLK, BLK)] = normed[rows, :].astype(F32).T.astype(BF16)
+                ksend[b, p - 1] = part[:, :HD]
+                k_copy(b, p).start()
+                vsend[b, p - 1] = part[:, HD:].astype(BF16)
+                v_copy(b, p).start()
+    for c in q_loads:
+        c.wait()
+
+    def rot_query(h, carry):
+        v = qs[h].astype(F32)
+        qr[h] = (v * cosv[...] + swap_halves(v) * sinv[...]).astype(BF16)
+        return carry
+
+    lax.fori_loop(0, HEADS, rot_query, 0)
+
     for c in c_loads:
         c.wait()
 
@@ -313,12 +324,12 @@
 
     def finish_grads(part):
         rows = pl.ds(0, BLK) if part == 0 else pl.ds(BLK, ROWS - BLK)
-        dk = dk_acc[rows, :]
+        dk = dk_acc[:, rows].T
         dkv[t, rows, pl.ds(0, HD)] = (
             dk * cosv[rows, :] - swap_halves(dk) * sinv[rows, :]
         ).astype(BF16)
-        dkv[t, rows, pl.ds(HD, HD)] = dv_acc[rows, :].astype(BF16)
-        for p in (3, 1, 2):
+        dkv[t, rows, pl.ds(HD, HD)] = dv_acc[:, rows].T.astype(BF16)
+        for p in (1, 2, 3):
             ag_copy(part, p).start()
 
     for b in range(NB):
@@ -327,14 +338,16 @@
         width = (b + 1) * BLK - low
         window = pl.ds(low, width)
         for p in range(1, 4):
-            kv_copy(b, p).wait_recv()
-        both = own_kv[b]
+            k_copy(b, p).wait_recv()
+            v_copy(b, p).wait_recv()
+        key = own_kv[b, :, :HD]
+        val = own_kv[b, :, HD:]
         for p in range(1, 4):
-            both = both + rbuf[b, p - 1].astype(F32)
-        both = both.astype(BF16)
-        key = both[:, :HD].astype(F32)
+            key = key + krecv[b, p - 1]
+            val = val + vrecv[b, p - 1].astype(F32)
+        key = key.astype(BF16).astype(F32)
         krot[rows, :] = (key * cosv[rows, :] + swap_halves(key) * sinv[rows, :]).astype(BF16)
-        vals[rows, :] = both[:, HD:]
+        vals[rows, :] = val.astype(BF16)
         q_index = lax.broadcasted_iota(jnp.int32, (BLK, width), 0) + b * BLK
         k_index = lax.broadcasted_iota(jnp.int32, (BLK, width), 1) + low
         same = segc[rows, :] == segr[:, low:low + width]
@@ -359,8 +372,8 @@
             gq[heads, rows, :] = (
                 dq * cosv[rows, :][None] - swap_halves(dq) * sinv[rows, :][None]
             ).astype(BF16)
-            dk_acc[window, :] += dot_tn(ds, qg)
-            dv_acc[window, :] += dot_tn(pb, cg)
+            dk_acc[:, window] += dot_tn(qg, ds)
+            dv_acc[:, window] += dot_tn(cg, pb)
             return carry
 
         lax.fori_loop(0, HEADS // GH, group, 0)
@@ -382,13 +395,14 @@
         )
 
     def partials(p):
-        for zt in range(ZS):
-            far = nt[pl.ds((2 * zt + other) * SH, SH), :]
-            csend[p, zt] = dot_nn(far, dkv[peers[p]]).astype(BF16)
+        dkvt[...] = dkv[peers[p]].astype(F32).T.astype(BF16)
+        for zt in (3, 0, 2, 1):
+            far = normed[:, pl.ds(pl.multiple_of((2 * zt + other) * SH, SH), SH)]
+            csend[p, zt] = dot_nn(dkvt[...], far).astype(BF16)
             cx_copy(p, zt).start()
-        for zt in range(ZS):
-            near = nt[pl.ds((2 * zt + core) * SH, SH), :]
-            own[p, zt] = dot_nn(near, dkv[peers[p]])
+        for zt in (3, 0, 2, 1):
+            near = normed[:, pl.ds(pl.multiple_of((2 * zt + core) * SH, SH), SH)]
+            own[p, zt] = dot_nn(dkvt[...], near)
 
     def pair_sums(p):
         for zt in (3, 0, 2, 1):
@@ -418,21 +432,28 @@
                 zsend[p, zt] = own[p, zt].astype(BF16)
                 left_copy(p, zt).start()
 
+    def relay_right(p, zt):
+        right_copy(p, zt).wait_recv()
+        zsend[p, zt] = (own[p, zt] + zfl[p, zt].astype(F32)).astype(BF16)
+        right_copy(p, zt).start()
+
+    def relay_left(p, zt):
+        left_copy(p, zt).wait_recv()
+        zsend[p, zt] = (own[p, zt] + zfr[p, zt].astype(F32)).astype(BF16)
+        left_copy(p, zt).start()
+
     def middle_sends(p):
-        for k in range(ZS - 1):
-            zt = ZS - 1 - k
-
-            @pl.when((z > 0) & (z < zt))
-            def _():
-                right_copy(p, zt).wait_recv()
-                zsend[p, zt] = (own[p, zt] + zfl[p, zt].astype(F32)).astype(BF16)
-                right_copy(p, zt).start()
-
-            @pl.when((z < ZS - 1) & (z > k))
-            def _():
-                left_copy(p, k).wait_recv()
-                zsend[p, k] = (own[p, k] + zfr[p, k].astype(F32)).astype(BF16)
-                left_copy(p, k).start()
+        @pl.when(z == 1)
+        def _():
+            relay_right(p, 3)
+            relay_right(p, 2)
+            relay_left(p, 0)
+
+        @pl.when(z == 2)
+        def _():
+            relay_left(p, 0)
+            relay_left(p, 1)
+            relay_right(p, 3)
 
     partials(0)
     pair_sums(0)
@@ -441,7 +462,6 @@
         ag_wait(0, p)
         ag_wait(1, p)
         partials(p)
-    for p in range(1, 4):
         pair_sums(p)
         end_sends(p)
 
@@ -513,6 +533,7 @@
                 if zt < ZS - 1:
                     left_copy(p, zt).wait_recv()
                     res = res + zfr[p, zt].astype(F32)
+                res = res.T
                 cols = pl.ds(pl.multiple_of(peers[p] * HD, HD), HD)
                 gkv[:, cols] = res[:, :HD]
                 gvv[:, cols] = res[:, HD:]
@@ -527,7 +548,8 @@
         ag_copy(0, p).wait_send()
         ag_copy(1, p).wait_send()
         for b in range(NB):
-            kv_copy(b, p).wait_send()
+            k_copy(b, p).wait_send()
+            v_copy(b, p).wait_send()
     for k in range(1, 2 * ZS):
         gain_copy(k).wait_send()
     for p in range(4):
@@ -539,6 +561,33 @@
                 right_copy(p, zt).wait_send()
     for c in outs + [gh_out, gk_out, gv_out]:
         c.wait()
+
+
+def store_kernel(*refs):
+    ins, outs, sem = refs[:6], refs[6:12], refs[12]
+    copies = []
+    for src, dst, cuts in zip(ins, outs, (2, 4, 2, 1, 1, 1)):
+        step = src.shape[0] // cuts
+        for k in range(cuts):
+            rows = pl.ds(k * step, step)
+            copies.append(pltpu.make_async_copy(src.at[rows], dst.at[rows], sem.at[len(copies)]))
+    for c in copies:
+        c.start()
+    for c in copies:
+        c.wait()
+
+
+def store_outputs(arrays):
+    hbm = pl.BlockSpec(memory_space=pl.ANY)
+    return pl.pallas_call(
+        store_kernel,
+        out_shape=tuple(jax.ShapeDtypeStruct(a.shape, a.dtype) for a in arrays),
+        in_specs=[hbm] * 6,
+        out_specs=(hbm,) * 6,
+        scratch_shapes=[pltpu.SemaphoreType.DMA((11,))],
+        compiler_params=pltpu.CompilerParams(vmem_limit_bytes=58 * 1024 * 1024),
+        name="store_outputs",
+    )(*arrays)
 
 
 def fused_body(hidden_in, norm_gain, key_weight, value_weight, queries, segments, cotangent):
@@ -547,6 +596,7 @@
     freq = jnp.asarray(np.concatenate([freq, freq])[None, :])
     vmem = pl.BlockSpec(memory_space=pltpu.VMEM)
     hbm = pl.BlockSpec(memory_space=pl.ANY)
+    pinned = pl.BlockSpec(memory_space=pl.ANY)
     dma = pltpu.SemaphoreType.DMA
     V = pltpu.VMEM
     outs = pl.pallas_call(
@@ -559,7 +609,7 @@
             jax.ShapeDtypeStruct((SH, KVH * HD), F32),
             jax.ShapeDtypeStruct((1, SH), F32),
         ),
-        in_specs=[hbm, vmem, hbm, hbm, hbm, vmem, hbm, vmem],
+        in_specs=[pinned] * 8,
         out_specs=(hbm, hbm, hbm, hbm, hbm, vmem),
         scratch_shapes=[
             V((ROWS, FEAT), BF16),
@@ -572,15 +622,20 @@
             V((ROWS, 1), F32),
             V((ROWS, 1), F32),
             V((ROWS, FEAT), BF16),
-            V((FEAT, ROWS), BF16),
+            V((KV, ROWS), BF16),
+            V((1, FEAT), F32),
+            V((1, ROWS), jnp.int32),
+            V((1, HD), F32),
             V((4, 8, ROWS), F32),
-            V((NB, 3, BLK, KV), KV_SEND),
-            V((NB, 3, BLK, KV), KV_SEND),
+            V((NB, 3, BLK, HD), F32),
+            V((NB, 3, BLK, HD), BF16),
+            V((NB, 3, BLK, HD), F32),
+            V((NB, 3, BLK, HD), BF16),
             V((NB, BLK, KV), F32),
             V((ROWS, HD), BF16),
             V((ROWS, HD), BF16),
-            V((ROWS, HD), F32),
-            V((ROWS, HD), F32),
+            V((HD, ROWS), F32),
+            V((HD, ROWS), F32),
             V((HEADS, ROWS, HD), BF16),
             V((HEADS, ROWS, HD), BF16),
             V((KVH, ROWS, KV), BF16),
@@ -589,18 +644,18 @@
             V((4, 8, ROWS), F32),
             V((2 * ZS, 8, SH), F32),
             V((2 * ZS, 8, SH), F32),
-            V((4, ZS, SH, KV), BF16),
-            V((4, ZS, SH, KV), BF16),
-            V((4, ZS, SH, KV), F32),
-            V((4, ZS, SH, KV), BF16),
-            V((4, ZS, SH, KV), BF16),
-            V((4, ZS, SH, KV), BF16),
+            V((4, ZS, KV, SH), BF16),
+            V((4, ZS, KV, SH), BF16),
+            V((4, ZS, KV, SH), F32),
+            V((4, ZS, KV, SH), BF16),
+            V((4, ZS, KV, SH), BF16),
+            V((4, ZS, KV, SH), BF16),
             V((SH, KVH * HD), F32),
             V((SH, KVH * HD), F32),
             V((ROWS, FEAT), BF16),
-            dma((25,)), dma((2 * HEADS + 3,)),
+            dma((28,)), dma((2 * HEADS + 3,)),
             dma((3,)), dma((3,)),
-            dma((NB, 3)), dma((NB, 3)),
+            dma((2, NB, 3)), dma((2, NB, 3)),
             dma((2, 3)), dma((2, 3)),
             dma((3,)), dma((3,)),
             dma((2 * ZS,)), dma((2 * ZS,)),
@@ -608,13 +663,14 @@
             dma((4, ZS)), dma((4, ZS)), dma((4, ZS)),
         ],
         compiler_params=pltpu.CompilerParams(
-            collective_id=0, has_side_effects=True, vmem_limit_bytes=56 * 1024 * 1024
+            collective_id=0, has_side_effects=True, vmem_limit_bytes=58 * 1024 * 1024
         ),
         name="fused_block",
     )(
         hidden_in, norm_gain[None, :], key_weight, value_weight, queries, segments, cotangent,
         freq,
     )
+    outs = store_outputs(outs)
     return outs[:5] + (outs[5][0],)
 
 

time: 114 us -> 241 us (2.11)
  Pallas kernels: 106 us -> 240 us
  local copies, waits for them, and re-layouts: 7.9 us -> 0 us
    pallas_call x0 -> x1, Pallas kernels: none -> 160 us  [store_outputs(): pl.pallas_call(store_kernel, out_shape=tuple((jax.ShapeDtypeStruct(a.shap...]
    pallas_call x1, Pallas kernels: 106 us -> 80.3 us  [fused_body(): pl.pallas_call(fused_kernel, out_shape=(jax.ShapeDtypeStruct((ROWS, HEADS...]
    unnamed x16 -> x0, local copies, waits for them, and re-layouts: 7.9 us -> none
where the time goes in v2:
time: 241 us
  Pallas kernels  240 us (100%)
    pallas_call x1, Pallas kernels, store_outputs(): pl.pallas_call(store_kernel, out_shape=tuple((jax.ShapeDtypeStruct(a.shap...  160 us
    pallas_call x1, Pallas kernels, fused_body(): pl.pallas_call(fused_kernel, out_shape=(jax.ShapeDtypeStruct((ROWS, HEADS...  80.3 us

profile of v2, /device:TPU:0, one launch (start us, length us, event | category | flops | bytes accessed | tf_op | source)
XLA Modules:
  0.0 241.2 jit_solution(5269309038098857515)
XLA Ops:
  0.6 80.3 %fused_block.1 = (bf16[512,1024]{1,0:T(8,128)(2,1)}, bf16[512,2048]{1,0:T(8,128)(2,1)}, bf16[512,1024]{1,0:T(8,128)(2,1)}, f32[256,512]{1,0:T(8,128)}, f32[256,512]{1,0:T(8,128)}, /*index=5*/f32[1,256]{1,0:T(1,128)}) custom-call(bf16[512,2048]{1,0:T(8,128)(2,1)} %hid_h.1, f32[1,2048]{1,0:T(1,128)} %bitcast.2, bf16[2048,512]{1,0:T(8,128)(2,1)} %kw_h.1, ...), custom_call_target="tpu_custom_call" | custom-call | tf_op jit(solution)/shard_map/fused_block/pallas_call | solution.py:602
  81.0 160.1 %store_outputs.1 = (bf16[512,1024]{1,0:T(8,128)(2,1)}, bf16[512,2048]{1,0:T(8,128)(2,1)}, bf16[512,1024]{1,0:T(8,128)(2,1)}, f32[256,512]{1,0:T(8,128)}, f32[256,512]{1,0:T(8,128)}, /*index=5*/f32[1,256]{1,0:T(1,128)}) custom-call(bf16[512,1024]{1,0:T(8,128)(2,1)} %get-tuple-element.18.refs_0_, bf16[512,2048]{1,0:T(8,128)(2,1)} %get-tuple-element.19.refs_1_, ...), custom_call_target="tpu_custom_call" | custom-call | tf_op jit(solution)/shard_map/store_outputs/pallas_call | solution.py:582

commit v3 on v2

--- a/solution.py
+++ b/solution.py
@@ -564,17 +564,22 @@
 
 
 def store_kernel(*refs):
-    ins, outs, sem = refs[:6], refs[6:12], refs[12]
-    copies = []
-    for src, dst, cuts in zip(ins, outs, (2, 4, 2, 1, 1, 1)):
+    ins, outs, bufs, in_sem, out_sem = refs[:6], refs[6:12], refs[12:18], refs[18], refs[19]
+    reads, writes = [], []
+    for src, buf, dst, cuts in zip(ins, bufs, outs, (2, 4, 2, 1, 1, 1)):
         step = src.shape[0] // cuts
         for k in range(cuts):
             rows = pl.ds(k * step, step)
-            copies.append(pltpu.make_async_copy(src.at[rows], dst.at[rows], sem.at[len(copies)]))
-    for c in copies:
+            n = len(reads)
+            reads.append(pltpu.make_async_copy(src.at[rows], buf.at[rows], in_sem.at[n]))
+            writes.append(pltpu.make_async_copy(buf.at[rows], dst.at[rows], out_sem.at[n]))
+    for c in reads:
         c.start()
-    for c in copies:
-        c.wait()
+    for r, w in zip(reads, writes):
+        r.wait()
+        w.start()
+    for w in writes:
+        w.wait()
 
 
 def store_outputs(arrays):
@@ -584,7 +589,8 @@
         out_shape=tuple(jax.ShapeDtypeStruct(a.shape, a.dtype) for a in arrays),
         in_specs=[hbm] * 6,
         out_specs=(hbm,) * 6,
-        scratch_shapes=[pltpu.SemaphoreType.DMA((11,))],
+        scratch_shapes=[pltpu.VMEM(a.shape, a.dtype) for a in arrays]
+        + [pltpu.SemaphoreType.DMA((11,)), pltpu.SemaphoreType.DMA((11,))],
         compiler_params=pltpu.CompilerParams(vmem_limit_bytes=58 * 1024 * 1024),
         name="store_outputs",
     )(*arrays)

time: 241 us -> 86 us (0.36)
  Pallas kernels: 240 us -> 85.1 us
    pallas_call x1, Pallas kernels: 160 us -> 4.73 us  [store_outputs(): pl.pallas_call(store_kernel, out_shape=tuple((jax.ShapeDtypeStruct(a.shap...]
where the time goes in v3:
time: 86 us; the launch traced here: 85.9 us
  Pallas kernels  85.1 us (99%)
    pallas_call x1, Pallas kernels, fused_body(): pl.pallas_call(fused_kernel, out_shape=(jax.ShapeDtypeStruct((ROWS, HEADS...  80.3 us
    pallas_call x1, Pallas kernels, store_outputs(): pl.pallas_call(store_kernel, out_shape=tuple((jax.ShapeDtypeStruct(a.shap...  4.73 us

profile of v3, /device:TPU:0, one launch (start us, length us, event | category | flops | bytes accessed | tf_op | source)
XLA Modules:
  0.0 85.9 jit_solution(631226837572313879)
XLA Ops:
  0.6 80.3 %fused_block.1 = (bf16[512,1024]{1,0:T(8,128)(2,1)}, bf16[512,2048]{1,0:T(8,128)(2,1)}, bf16[512,1024]{1,0:T(8,128)(2,1)}, f32[256,512]{1,0:T(8,128)}, f32[256,512]{1,0:T(8,128)}, /*index=5*/f32[1,256]{1,0:T(1,128)}) custom-call(bf16[512,2048]{1,0:T(8,128)(2,1)} %hid_h.1, f32[1,2048]{1,0:T(1,128)} %bitcast.2, bf16[2048,512]{1,0:T(8,128)(2,1)} %kw_h.1, ...), custom_call_target="tpu_custom_call" | custom-call | tf_op jit(solution)/shard_map/fused_block/pallas_call | solution.py:608
  81.0 4.7 %store_outputs.1 = (bf16[512,1024]{1,0:T(8,128)(2,1)}, bf16[512,2048]{1,0:T(8,128)(2,1)}, bf16[512,1024]{1,0:T(8,128)(2,1)}, f32[256,512]{1,0:T(8,128)}, f32[256,512]{1,0:T(8,128)}, /*index=5*/f32[1,256]{1,0:T(1,128)}) custom-call(bf16[512,1024]{1,0:T(8,128)(2,1)} %get-tuple-element.18.refs_0_, bf16[512,2048]{1,0:T(8,128)(2,1)} %get-tuple-element.19.refs_1_, ...), custom_call_target="tpu_custom_call" | custom-call | tf_op jit(solution)/shard_map/store_outputs/pallas_call | solution.py:587
